TPU v7x, 128 devices: a whole 4x4x4 slice. The times are simulated.
128 devices in a mesh: hst: 8 (over y, core), chip: 16 (over z, x).
Axes of the slice: x: 4, y: 4, z: 4, core: 2. Of those that a mesh axis runs over, the one named last changes fastest.
Arguments:
- inputs: bfloat16 [128, 4096], P(('hst', 'chip')), may hold values from -6 to 6
- values: bfloat16 [131072, 4096], P(('hst', 'chip')), may hold values from -6 to 6
- slots: int32 [128, 4, 32], P(('hst', 'chip')), may hold values from 0 to 131071, as said below
- weights: bfloat16 [128, 4, 32], P(('hst', 'chip')), may hold values from -0.59765625 to 0.59765625
Outputs:
- mixed: bfloat16 [128, 4096], P(('hst', 'chip'))
Inputs may be any that keep to these rules, and one draw needn't show every extreme that they name: `slots`: of the 128 picks of the rows on one device, at most 4 name value rows held by one device; some devices' value rows are named that often by every device.
All inputs are finite; a program needn't handle non-finite values.
Results may differ from a plain program's by a relative error of at most 0.009.
Values may be sent and summed in bfloat16 or wider, within the bound.
No kernel may reach another device: no remote copies, remote signals or barrier semaphores. Data moves between devices by JAX's collectives and lax.ppermute only.
A program may use at most 64 MiB of HBM per device.

v0:
```python
import jax
import jax.numpy as jnp
from jax import lax
from jax.sharding import PartitionSpec as P


def body(inputs, values, slots, weights):
    n_outer = lax.axis_size("hst")
    n_inner = lax.axis_size("chip")
    owners = n_outer * n_inner
    slot_dev = values.shape[0]
    width = values.shape[1]
    q_dev = inputs.shape[0]
    picks = slots.size
    cap = 4 * picks // owners
    flat_slots = slots.reshape(-1)
    flat_weights = weights.reshape(-1)
    owner_id = flat_slots // slot_dev
    local_row = flat_slots % slot_dev
    query_row = jnp.arange(picks, dtype=jnp.int32) // (picks // q_dev)
    onehot = (owner_id[:, None] == jnp.arange(owners, dtype=jnp.int32)[None, :]).astype(jnp.int32)
    ranking = jnp.sum(jnp.cumsum(onehot, axis=0) * onehot, axis=1) - 1
    placing = owner_id * cap + ranking
    packed = jnp.zeros((owners * cap,), jnp.int32).at[placing].set(query_row * slot_dev + local_row)
    sent_weights = jnp.zeros((owners * cap,), jnp.bfloat16).at[placing].set(flat_weights)
    got_packed, got_weights = (
        lax.all_to_all(
            packed.reshape(owners, cap), ("hst", "chip"), split_axis=0, concat_axis=0, tiled=True
        ),
        lax.all_to_all(
            sent_weights.reshape(owners, cap),
            ("hst", "chip"),
            split_axis=0,
            concat_axis=0,
            tiled=True,
        ),
    )
    got_rows = got_packed % slot_dev
    got_query = got_packed // slot_dev
    value_rows = jnp.take(values, got_rows.reshape(-1), axis=0).reshape(owners, cap, width)
    matches = got_query[:, None, :] == jnp.arange(q_dev, dtype=jnp.int32)[None, :, None]
    weight_table = jnp.where(matches, got_weights[:, None, :], jnp.zeros((), jnp.bfloat16))
    partials = jnp.einsum(
        "sqc,scd->sqd", weight_table, value_rows, preferred_element_type=jnp.float32
    )
    returned = lax.all_to_all(
        partials.astype(jnp.bfloat16), ("hst", "chip"), split_axis=0, concat_axis=0, tiled=True
    ).astype(partials.dtype)
    memory = jnp.sum(returned, axis=0)
    return (inputs.astype(jnp.float32) + memory).astype(jnp.bfloat16)


def solution(mesh):
    in_specs = (
        P(("hst", "chip"), None),
        P(("hst", "chip"), None),
        P(("hst", "chip"), None, None),
        P(("hst", "chip"), None, None),
    )
    out_specs = P(("hst", "chip"), None)
    return jax.shard_map(body, mesh=mesh, in_specs=in_specs, out_specs=out_specs, check_vma=False)
```

profile of v0, /device:TPU:1, one launch (start us, length us, event | category | flops | bytes accessed | tf_op | source)
XLA Modules:
  0.0 97.3 jit_solution(17754980926172336951)
XLA Ops:
  0.0 0.8 reshape.204
  0.8 0.8 reshape.203
  2.0 1.0 %scatter_custom_fusion = s32[512]{0:T(512)S(1)} fusion(s32[128]{0:T(128)S(1)} %fusion.12, s32[128]{0:T(128)S(1)} %get-tuple-element.5, s32[]{:T(128)} %constant.80.clone.1), kind=kCustom, calls=%fused_computation.45 | custom fusion | bytes 2052 | tf_op jit(solution)/shard_map/scatter | solution.py:24
  3.0 0.7 all_to_all.19
  3.7 11.5 %all-to-all-start = ((s32[128,1,4]{2,1,0:T(1,128)}), s32[128,1,4]{2,1,0:T(1,128)S(1)}, u32[]{:S(2)}, u32[]{:S(2)}) async-start(s32[128,1,4]{2,1,0:T(1,128)} %bitcast.2), calls=%async_computation | async-start | bytes 131072 | tf_op jit(solution)/shard_map/all_to_all | solution.py:27
  15.2 0.8 reshape.227
  16.0 1.3 %scatter_custom_fusion.1 = bf16[512]{0:T(512)(128)(2,1)S(1)} fusion(s32[128]{0:T(128)S(1)} %fusion.12, bf16[128]{0:T(256)(128)(2,1)S(1)} %reshape.227, bf16[]{:T(256)} %constant.90.clone.1), kind=kCustom, calls=%fused_computation.51 | custom fusion | bytes 1026 | tf_op jit(solution)/shard_map/scatter | solution.py:25
  17.3 0.8 all_to_all.26
  18.1 6.9 %all-to-all-done = s32[128,1,4]{2,1,0:T(1,128)S(1)} async-done(((s32[128,1,4]{2,1,0:T(1,128)}), s32[128,1,4]{2,1,0:T(1,128)S(1)}, u32[]{:S(2)}, u32[]{:S(2)}) %all-to-all-start) | async-done | bytes 2080 | tf_op jit(solution)/shard_map/all_to_all | solution.py:27
  25.0 4.3 %all-to-all-start.1 = ((bf16[128,1,4]{2,1,0:T(2,128)(2,1)}), bf16[128,1,4]{2,1,0:T(2,128)(2,1)S(1)}, u32[]{:S(2)}, u32[]{:S(2)}) async-start(bf16[128,1,4]{2,1,0:T(2,128)(2,1)} %all_to_all.26), calls=%async_computation.1 | async-start | bytes 131072 | tf_op jit(solution)/shard_map/all_to_all | solution.py:30
  29.3 9.7 %all-to-all-done.1 = bf16[128,1,4]{2,1,0:T(2,128)(2,1)S(1)} async-done(((bf16[128,1,4]{2,1,0:T(2,128)(2,1)}), bf16[128,1,4]{2,1,0:T(2,128)(2,1)S(1)}, u32[]{:S(2)}, u32[]{:S(2)}) %all-to-all-start.1) | async-done | bytes 1056 | tf_op jit(solution)/shard_map/all_to_all | solution.py:30
  39.5 0.5 broadcast.276
  40.0 0.8 reduce.4
  41.1 13.0 %gather_fusion = bf16[512,4096]{1,0:T(8,128)(2,1)} fusion(bf16[1024,4096]{1,0:T(8,128)(2,1)} %param.5, s32[1024]{0:T(1024)S(1)} %pad_clamp_fusion), kind=kCustom, calls=%fused_computation | custom fusion | bytes 8390656 | tf_op jit(solution)/shard_map/jit(_take)/gather | solution.py:40
  54.2 7.2 %gather.7 = bf16[128,4,4096]{2,1,0:T(4,128)(2,1)} reshape(bf16[512,4096]{1,0:T(8,128)(2,1)} %gather_fusion) | data formatting | bytes 8388608 | tf_op jit(solution)/shard_map/jit(_take)/gather | solution.py:40
  61.4 4.6 %fusion = bf16[128,1,4096]{2,1,0:T(2,128)(2,1)S(1)} fusion(bf16[128,4,1]{1,2,0:T(2,128)(2,1)S(1)} %copy.11, bf16[128,4,4096]{2,1,0:T(4,128)(2,1)} %gather.7, pred[128,4]{1,0:T(8,128)(4,1)S(1)} %compare_and_fusion), kind=kOutput, calls=%fused_computation.3 | convolution fusion | flops 6291456 | bytes 5244416 | tf_op jit(solution)/shard_map/sqc,scd->sqd/dot_general | solution.py:43
  66.0 1.1 %copy.16 = bf16[128,1,4096]{2,0,1:T(8,128)(2,1)S(1)} copy(bf16[128,1,4096]{2,1,0:T(2,128)(2,1)S(1)} %fusion) | data formatting | bytes 2097152 | tf_op jit(solution)/shard_map/sqc,scd->sqd/dot_general | solution.py:43
  67.1 0.5 broadcast.277
  67.6 1.4 %reduce.5 = bf16[128,4096]{1,0:T(8,128)(2,1)S(1)} reduce(bf16[128,1,4096]{2,0,1:T(8,128)(2,1)S(1)} %copy.16, bf16[]{:T(256)} %broadcast.277), dimensions={1}, to_apply=%copy.10.reduce_sub_computation | reduce | bytes 2097154 | tf_op jit(solution)/shard_map/convert_element_type | solution.py:47
  69.0 0.8 reshape.246
  69.9 23.4 %all_to_all.30 = bf16[128,2,2048]{2,1,0:T(2,128)(2,1)S(1)} all-to-all(bf16[128,2,2048]{2,1,0:T(2,128)(2,1)S(1)} %reshape.246), channel_id=1, replica_groups=mesh['hst'=8,'chip'=16] {'hst','chip'}, dimensions={0} | all-to-all | bytes 2097152 | tf_op jit(solution)/shard_map/all_to_all | solution.py:46
  93.2 1.0 %reshape.247 = bf16[128,1,4096]{2,1,0:T(2,128)(2,1)S(1)} reshape(bf16[128,2,2048]{2,1,0:T(2,128)(2,1)S(1)} %all_to_all.30) | data formatting | bytes 2097152
  94.3 2.4 %convert_reduce_fusion = f32[4096]{0:T(1024)S(1)} fusion(bf16[128,1,4096]{2,1,0:T(2,128)(2,1)S(1)} %reshape.247), kind=kLoop, calls=%fused_computation.7 | loop fusion | flops 1044480 | bytes 1064960 | tf_op jit(solution)/shard_map/reduce_sum | solution.py:49
  96.7 0.6 add_convert_fusion
  (14 shorter events, 1.2 us)
Async XLA Ops:
  3.7 21.3 %all-to-all-start = ((s32[128,1,4]{2,1,0:T(1,128)}), s32[128,1,4]{2,1,0:T(1,128)S(1)}, u32[]{:S(2)}, u32[]{:S(2)}) async-start(s32[128,1,4]{2,1,0:T(1,128)} %bitcast.2), calls=%async_computation | async-start | bytes 131072 | tf_op jit(solution)/shard_map/all_to_all | solution.py:27
  25.0 14.1 %all-to-all-start.1 = ((bf16[128,1,4]{2,1,0:T(2,128)(2,1)}), bf16[128,1,4]{2,1,0:T(2,128)(2,1)S(1)}, u32[]{:S(2)}, u32[]{:S(2)}) async-start(bf16[128,1,4]{2,1,0:T(2,128)(2,1)} %all_to_all.26), calls=%async_computation.1 | async-start | bytes 131072 | tf_op jit(solution)/shard_map/all_to_all | solution.py:30
  69.8 26.8 %copy-start = (bf16[1,4096]{1,0:T(2,128)(2,1)S(1)}, bf16[1,4096]{1,0:T(2,128)(2,1)}, u32[]{:S(2)}) copy-start(bf16[1,4096]{1,0:T(2,128)(2,1)} %param.4) | copy-start | bytes 24580
where the time goes:
time: 97.8 us; the launch traced here: 97.3 us
  local copies, waits for them, and re-layouts  30.7 us (31%)
  blocking collectives  23.4 us (24%)
  waiting for transfers between devices  16.6 us (17%)
  starting transfers between devices  15.8 us (16%)
  other arithmetic  6.12 us (6%)
  matrix products  4.6 us (5%)
    all_to_all x1, blocking collectives, body(): lax.all_to_all(partials.astype(jnp.bfloat16), ('hst', 'chip'), split_axis...  23.4 us
    gather x2, local copies, waits for them, and re-layouts, body(): jnp.take(values, got_rows.reshape(-1), axis=0).reshape(owners, cap, width)  20.2 us
    all_to_all x1, starting transfers between devices, body(): lax.all_to_all(packed.reshape(owners, cap), ('hst', 'chip'), split_axis=0...  11.5 us
    all_to_all x1, waiting for transfers between devices, body(): lax.all_to_all(sent_weights.reshape(owners, cap), ('hst', 'chip'), split_...  9.73 us
    all_to_all x1, waiting for transfers between devices, body(): lax.all_to_all(packed.reshape(owners, cap), ('hst', 'chip'), split_axis=0...  6.91 us
    dot_general x1, matrix products, body(): jnp.einsum('sqc,scd->sqd', weight_table, value_rows, preferred_element_ty...  4.6 us
    all_to_all x1, starting transfers between devices, body(): lax.all_to_all(sent_weights.reshape(owners, cap), ('hst', 'chip'), split_...  4.29 us
    reduce_sum x1, other arithmetic, body(): memory = jnp.sum(returned, axis=0)  2.4 us
  transfers between devices with their start and end apart: 2, of which 2 were waited for; matrix products, arithmetic and copies ran while one was open for 2% of the time, Pallas kernels for 0%

commit v1 on v0

v1 whole, which is shorter than its diff:
```python
import jax
import jax.numpy as jnp
from jax import lax
from jax.experimental import pallas as pl
from jax.experimental.pallas import tpu as pltpu
from jax.sharding import Mesh, PartitionSpec as P

AXES = ("y", "core", "z", "x")
CHIPS = ("x", "z", "y")
GROUP = ("core", *CHIPS)
LANES = 128
MIB = 1024 * 1024


def request_kernel(
    owners, cap, slots_hbm, weights_hbm, values_hbm, out_ref, slots_ref, weights_ref, sems
):
    slot_dev = values_hbm.shape[0]
    copies = [
        pltpu.make_async_copy(slots_hbm, slots_ref, sems.at[0]),
        pltpu.make_async_copy(weights_hbm, weights_ref, sems.at[1]),
    ]
    for copy in copies:
        copy.start()
    for copy in copies:
        copy.wait()
    heads = slots_ref.shape[1]
    slots = slots_ref[0]
    weights = weights_ref[0].astype(jnp.float32)
    slots = jnp.concatenate([slots[h : h + 1] for h in range(heads)], axis=1)
    weights = jnp.concatenate([weights[h : h + 1] for h in range(heads)], axis=1)
    picks = slots.shape[1]
    owner = slots // slot_dev
    row = slots - owner * slot_dev
    low = row % 32
    high = row - low
    xs, zs, ys = (lax.axis_size(axis) for axis in CHIPS)
    y, core = owner // (2 * zs * xs), owner // (zs * xs) % 2
    z, x = owner // xs % zs, owner % xs
    owner = ((core * xs + x) * zs + z) * ys + y
    mine = owner == lax.broadcasted_iota(jnp.int32, (owners, picks), 0)
    before = lax.broadcasted_iota(jnp.int32, (picks, picks), 0) < lax.broadcasted_iota(
        jnp.int32, (picks, picks), 1
    )
    marks = jnp.where(mine, 1.0, 0.0).astype(jnp.bfloat16)
    earlier = jnp.dot(
        marks,
        jnp.where(before, 1.0, 0.0).astype(jnp.bfloat16),
        preferred_element_type=jnp.float32,
    )
    rank = jnp.sum(jnp.where(mine, earlier, 0.0), axis=0, keepdims=True).astype(jnp.int32)
    lane = lax.broadcasted_iota(jnp.int32, (LANES, picks), 0) - rank
    fields = jnp.where(
        lane == 0,
        high.astype(jnp.float32),
        jnp.where(
            lane == cap, low.astype(jnp.float32), jnp.where(lane == 2 * cap, weights, 0.0)
        ),
    )
    out_ref[...] = lax.dot_general(
        marks,
        fields.astype(jnp.bfloat16),
        (((1,), (1,)), ((), ())),
        preferred_element_type=jnp.float32,
    )


def half_kernel(cap, chunk, other, got_ref, slab_ref, out_ref, table):
    slot_dev, width = slab_ref.shape
    sources = got_ref.shape[0]
    core = lax.axis_index("core")
    core = 1 - core if other else core
    group = 16
    for n in range(sources // group):
        got = got_ref[pl.ds(n * group, group)]

        def spread(lane):
            return jnp.broadcast_to(got[:, lane : lane + 1], (group, LANES))

        rows = [spread(c) + spread(cap + c) for c in range(cap)]
        scales = [spread(2 * cap + c) for c in range(cap)]
        scales = [
            sum(jnp.where(rows[c] == rows[d], scales[d], 0.0) for d in range(cap)).astype(
                jnp.bfloat16
            )
            for c in range(cap)
        ]
        rows = [row.astype(jnp.int32).astype(jnp.int16) for row in rows]
        lane = lax.broadcasted_iota(jnp.int32, (group, LANES), 1)
        for k in range(slot_dev // LANES):
            at = (lane + k * LANES).astype(jnp.int16)
            weight = jnp.zeros((group, LANES), jnp.bfloat16)
            for c in range(cap):
                weight = jnp.where(at == rows[c], scales[c], weight)
            table[pl.ds(n * group, group), pl.ds(k * LANES, LANES)] = weight
    parts = chunk // LANES
    for n in range(width // 2 // chunk):
        columns = pl.ds(pl.multiple_of(core * (width // 2) + n * chunk, chunk), chunk)
        summed = jnp.dot(table[...], slab_ref[:, columns], preferred_element_type=jnp.float32)
        summed = summed.astype(out_ref.dtype)
        out_ref[:, pl.ds(n * parts, parts), :] = summed.reshape(sources, parts, LANES)


def add_kernel(got_ref, kept_ref, out_ref):
    out_ref[...] = (got_ref[...].astype(jnp.float32) + kept_ref[...]).astype(out_ref.dtype)


def sum_kernel(got_ref, inputs_ref, out_ref):
    sources, tiles, _ = got_ref.shape
    chips = sources // 2
    memory = jnp.concatenate(
        [
            jnp.sum(got_ref[pl.ds(core * chips, chips)].astype(jnp.float32), axis=0)
            for core in range(2)
        ],
        axis=0,
    )
    for j in range(2 * tiles):
        part = pl.ds(j * LANES, LANES)
        out_ref[:, part] = (inputs_ref[:, part].astype(jnp.float32) + memory[j : j + 1]).astype(
            jnp.bfloat16
        )


def body(inputs, values, slots, weights):
    owners = lax.axis_size(AXES)
    slot_dev, width = values.shape
    cap = 4 * slots.size // owners
    tiles = width // LANES
    chunk = 2048
    vmem = pl.BlockSpec(memory_space=pltpu.VMEM)
    hbm = pl.BlockSpec(memory_space=pltpu.HBM)

    def call(kernel, shapes, specs, name, scratch=()):
        return pl.pallas_call(
            kernel,
            out_shape=[pltpu.VMEM(*shape) for shape in shapes],
            in_specs=specs,
            out_specs=[vmem] * len(shapes),
            scratch_shapes=scratch,
            compiler_params=pltpu.CompilerParams(vmem_limit_bytes=24 * MIB),
            name=name,
        )

    constrain = pltpu.with_memory_space_constraint
    (packed,) = call(
        lambda *refs: request_kernel(owners, cap, *refs),
        [((owners, LANES), jnp.float32)],
        [hbm] * 3,
        "request",
        [
            pltpu.VMEM(slots.shape, slots.dtype),
            pltpu.VMEM(weights.shape, weights.dtype),
            pltpu.SemaphoreType.DMA((2,)),
        ],
    )(*[constrain(array, pltpu.HBM) for array in (slots, weights, values)])
    got = lax.all_to_all(
        packed.reshape(owners, 1, LANES), GROUP, split_axis=0, concat_axis=0, tiled=True
    ).reshape(owners, LANES)
    half = (owners, tiles // 2, LANES)
    slab = constrain(values, pltpu.VMEM)
    other, own = [
        call(
            lambda *refs, other=other: half_kernel(cap, chunk, other, *refs),
            [(half, jnp.bfloat16 if other else jnp.float32)],
            [vmem] * 2,
            "other_half" if other else "own_half",
            [pltpu.VMEM((owners, slot_dev), jnp.bfloat16)],
        )(got, slab)[0]
        for other in (True, False)
    ]
    swapped = lax.ppermute(other, "core", [(0, 1), (1, 0)])
    (partials,) = call(add_kernel, [(half, jnp.bfloat16)], [vmem] * 2, "add")(swapped, own)
    returned = lax.all_to_all(partials, GROUP, split_axis=0, concat_axis=0, tiled=True)
    return pl.pallas_call(
        sum_kernel,
        out_shape=jax.ShapeDtypeStruct(inputs.shape, jnp.bfloat16),
        in_specs=[vmem] * 2,
        out_specs=vmem,
        compiler_params=pltpu.CompilerParams(vmem_limit_bytes=24 * MIB),
        name="sum",
    )(returned, inputs)


def solution(mesh):
    hst, chip = mesh.devices.shape
    mesh = Mesh(mesh.devices.reshape(hst // 2, 2, 4, chip // 4), AXES)
    in_specs = (P(AXES, None), P(AXES, None), P(AXES, None, None), P(AXES, None, None))
    return jax.shard_map(
        body, mesh=mesh, in_specs=in_specs, out_specs=P(AXES, None), check_vma=False
    )
```

time: 97.8 us -> 43.7 us (0.45)
  local copies, waits for them, and re-layouts: 30.7 us -> 0.01 us
  waiting for transfers between devices: 16.6 us -> 0.35 us
  starting transfers between devices: 15.8 us -> 0.8 us
  blocking collectives: 23.4 us -> 38 us
  other arithmetic: 6.12 us -> 0 us
  matrix products: 4.6 us -> 0 us
  Pallas kernels: 0 us -> 4.37 us
    gather x2 -> x0, local copies, waits for them, and re-layouts: 20.2 us -> none  [body(): jnp.take(values, got_rows.reshape(-1), axis=0).reshape(owners, cap, width)]
    all_to_all x2 -> x0, waiting for transfers between devices: 16.6 us -> none  [the longest x1 9.73 us: body(): lax.all_to_all(sent_weights.reshape(owners, cap), ('hst', 'chip'), split_...]
    all_to_all x2 -> x0, starting transfers between devices: 15.8 us -> none  [the longest x1 11.5 us: body(): lax.all_to_all(packed.reshape(owners, cap), ('hst', 'chip'), split_axis=0...]
    all_to_all x1 -> x2, blocking collectives: 23.4 us -> 38 us  [the longest x1 20.8 us: body(): lax.all_to_all(packed.reshape(owners, 1, LANES), GROUP, split_axis=0, con...]
    dot_general x1 -> x0, matrix products: 4.6 us -> none  [body(): jnp.einsum('sqc,scd->sqd', weight_table, value_rows, preferred_element_ty...]
    pallas_call x0 -> x5, Pallas kernels: none -> 4.37 us  [the longest x2 2.28 us: body(): call(lambda *refs, other=other: half_kernel(cap, chunk, other, *refs), [(...]
    reduce_sum x2 -> x0, other arithmetic: 2.57 us -> none  [the longest x1 2.4 us: body(): memory = jnp.sum(returned, axis=0)]
    scatter x2 -> x0, local copies, waits for them, and re-layouts: 2.32 us -> none  [the longest x1 1.34 us: body(): jnp.zeros((owners * cap,), jnp.bfloat16).at[placing].set(flat_weights)]
  transfers between devices with their start and end apart: 2 -> 1, of which waited for: 2 -> 1; matrix products, arithmetic and copies ran while one was open for 2% -> 0% of each run, Pallas kernels for 0% -> 3%
where the time goes in v1:
time: 43.7 us; the launch traced here: 43.6 us
  blocking collectives  38 us (87%)
  Pallas kernels  4.37 us (10%)
  starting transfers between devices  0.8 us (2%)
    all_to_all x1, blocking collectives, body(): lax.all_to_all(packed.reshape(owners, 1, LANES), GROUP, split_axis=0, con...  20.8 us
    all_to_all x1, blocking collectives, body(): lax.all_to_all(partials, GROUP, split_axis=0, concat_axis=0, tiled=True)  17.2 us
    pallas_call x2, Pallas kernels, body(): call(lambda *refs, other=other: half_kernel(cap, chunk, other, *refs), [(...  2.28 us
    pallas_call x1, Pallas kernels, body(): call(lambda *refs: request_kernel(owners, cap, *refs), [((owners, LANES),...  1.27 us
  transfers between devices with their start and end apart: 1, of which 1 were waited for; matrix products, arithmetic and copies ran while one was open for 0% of the time, Pallas kernels for 3%

profile of v1, /device:TPU:1, one launch (start us, length us, event | category | flops | bytes accessed | tf_op | source)
XLA Modules:
  0.0 43.6 jit_solution(16341086937015151628)
XLA Ops:
  0.0 0.0 copy-start
  0.0 1.3 %request.1 = f32[128,128]{1,0:T(8,128)S(1)} custom-call(s32[1,4,32]{2,1,0:T(4,128)} %refs_0_.1, bf16[1,4,32]{2,1,0:T(4,128)(2,1)} %refs_1_.3, bf16[1024,4096]{1,0:T(8,128)(2,1)} %refs_1_.5), custom_call_target="tpu_custom_call" | custom-call | tf_op jit(solution)/shard_map/request/pallas_call | solution.py:146
  1.3 20.8 %all_to_all.10 = f32[128,1,128]{2,1,0:T(1,128)S(1)} all-to-all(f32[128,1,128]{2,1,0:T(1,128)S(1)} %bitcast.6), channel_id=1, replica_groups=mesh['y'=4,'core'=2,'z'=4,'x'=4] {'core','x','z','y'}, dimensions={0} | all-to-all | bytes 131072 | tf_op jit(solution)/shard_map/all_to_all | solution.py:157
  22.0 0.0 copy-done
  22.1 1.1 %other_half.1 = bf16[128,16,128]{2,1,0:T(8,128)(2,1)S(1)} custom-call(f32[128,128]{1,0:T(8,128)S(1)} %bitcast.4, bf16[1024,4096]{1,0:T(8,128)(2,1)S(1)} %copy-done), custom_call_target="tpu_custom_call" | custom-call | tf_op jit(solution)/shard_map/other_half/pallas_call | solution.py:163
  23.2 0.0 copy-start.1
  23.2 0.8 %collective-permute-start = (bf16[128,16,128]{2,1,0:T(8,128)(2,1)S(1)}, bf16[128,16,128]{2,1,0:T(8,128)(2,1)S(1)}, u32[]{:S(2)}, u32[]{:S(2)}) collective-permute-start(bf16[128,16,128]{2,1,0:T(8,128)(2,1)S(1)} %other_half.1), channel_id=1, source_target_pairs={{0,16},{16,0},{1,17},{17,1},{2,18},{18,2},{3,19},{19,3},{4,20},{20... | collective-permute-start | bytes 1572872 | tf_op jit(solution)/shard_map/ppermute | solution.py:172
  24.0 1.2 %own_half.1.kept_ref = f32[128,16,128]{2,1,0:T(8,128)S(1)} custom-call(f32[128,128]{1,0:T(8,128)S(1)} %bitcast.5, bf16[1024,4096]{1,0:T(8,128)(2,1)S(1)} %copy-done), custom_call_target="tpu_custom_call" | custom-call | tf_op jit(solution)/shard_map/own_half/pallas_call | solution.py:163
  25.2 0.3 collective-permute-done.got_ref
  25.5 0.1 add.1
  25.6 17.2 %all_to_all.11.got_ref = bf16[128,16,128]{2,1,0:T(8,128)(2,1)S(1)} all-to-all(bf16[128,16,128]{2,1,0:T(8,128)(2,1)S(1)} %add.1), channel_id=1, replica_groups=mesh['y'=4,'core'=2,'z'=4,'x'=4] {'core','x','z','y'}, dimensions={0} | all-to-all | bytes 1048576 | tf_op jit(solution)/shard_map/all_to_all | solution.py:174
  42.8 0.0 copy-done.1
  42.8 0.7 %sum.1 = bf16[1,4096]{1,0:T(2,128)(2,1)} custom-call(bf16[128,16,128]{2,1,0:T(8,128)(2,1)S(1)} %all_to_all.11.got_ref, bf16[1,4096]{1,0:T(2,128)(2,1)S(1)} %copy-done.1), custom_call_target="tpu_custom_call" | custom-call | tf_op jit(solution)/shard_map/sum/pallas_call | solution.py:175
Async XLA Ops:
  0.0 22.1 %copy-start = (bf16[1024,4096]{1,0:T(8,128)(2,1)S(1)}, bf16[1024,4096]{1,0:T(8,128)(2,1)}, u32[]{:S(2)}) copy-start(bf16[1024,4096]{1,0:T(8,128)(2,1)} %refs_1_.5) | copy-start | bytes 25165828
  23.2 19.7 %copy-start.1 = (bf16[1,4096]{1,0:T(2,128)(2,1)S(1)}, bf16[1,4096]{1,0:T(2,128)(2,1)}, u32[]{:S(2)}) copy-start(bf16[1,4096]{1,0:T(2,128)(2,1)} %inputs_ref.1) | copy-start | bytes 24580
  23.2 2.3 %collective-permute-start = (bf16[128,16,128]{2,1,0:T(8,128)(2,1)S(1)}, bf16[128,16,128]{2,1,0:T(8,128)(2,1)S(1)}, u32[]{:S(2)}, u32[]{:S(2)}) collective-permute-start(bf16[128,16,128]{2,1,0:T(8,128)(2,1)S(1)} %other_half.1), channel_id=1, source_target_pairs={{0,16},{16,0},{1,17},{17,1},{2,18},{18,2},{3,19},{19,3},{4,20},{20... | collective-permute-start | bytes 1572872 | tf_op jit(solution)/shard_map/ppermute | solution.py:172

commit v2 on v1

--- a/solution.py
+++ b/solution.py
@@ -110,16 +110,16 @@
     chips = sources // 2
     memory = jnp.concatenate(
         [
-            jnp.sum(got_ref[pl.ds(core * chips, chips)].astype(jnp.float32), axis=0)
+            sum(
+                jnp.sum(got_ref[pl.ds(core * chips + n, 8)].astype(jnp.float32), axis=0)
+                for n in range(0, chips, 8)
+            )
             for core in range(2)
         ],
         axis=0,
     )
-    for j in range(2 * tiles):
-        part = pl.ds(j * LANES, LANES)
-        out_ref[:, part] = (inputs_ref[:, part].astype(jnp.float32) + memory[j : j + 1]).astype(
-            jnp.bfloat16
-        )
+    memory = memory.reshape(1, 2 * tiles * LANES)
+    out_ref[...] = (inputs_ref[...].astype(jnp.float32) + memory).astype(jnp.bfloat16)
 
 
 def body(inputs, values, slots, weights):

time: 43.7 us -> 43.7 us (level)
  no operation moved by 1% of the time
where the time goes in v2:
time: 43.7 us; the launch traced here: 43.5 us
  blocking collectives  38 us (87%)
  Pallas kernels  4.34 us (10%)
  starting transfers between devices  0.8 us (2%)
    all_to_all x1, blocking collectives, body(): lax.all_to_all(packed.reshape(owners, 1, LANES), GROUP, split_axis=0, con...  20.8 us
    all_to_all x1, blocking collectives, body(): lax.all_to_all(partials, GROUP, split_axis=0, concat_axis=0, tiled=True)  17.2 us
    pallas_call x2, Pallas kernels, body(): call(lambda *refs, other=other: half_kernel(cap, chunk, other, *refs), [(...  2.28 us
    pallas_call x1, Pallas kernels, body(): call(lambda *refs: request_kernel(owners, cap, *refs), [((owners, LANES),...  1.27 us
  transfers between devices with their start and end apart: 1, of which 1 were waited for; matrix products, arithmetic and copies ran while one was open for 0% of the time, Pallas kernels for 3%

profile of v2, /device:TPU:1, one launch (start us, length us, event | category | flops | bytes accessed | tf_op | source)
XLA Modules:
  0.0 43.5 jit_solution(4217717502249562033)
XLA Ops:
  0.0 0.0 copy-start
  0.0 1.3 %request.1 = f32[128,128]{1,0:T(8,128)S(1)} custom-call(s32[1,4,32]{2,1,0:T(4,128)} %refs_0_.1, bf16[1,4,32]{2,1,0:T(4,128)(2,1)} %refs_1_.3, bf16[1024,4096]{1,0:T(8,128)(2,1)} %refs_1_.5), custom_call_target="tpu_custom_call" | custom-call | tf_op jit(solution)/shard_map/request/pallas_call | solution.py:146
  1.3 20.8 %all_to_all.10 = f32[128,1,128]{2,1,0:T(1,128)S(1)} all-to-all(f32[128,1,128]{2,1,0:T(1,128)S(1)} %bitcast.6), channel_id=1, replica_groups=mesh['y'=4,'core'=2,'z'=4,'x'=4] {'core','x','z','y'}, dimensions={0} | all-to-all | bytes 131072 | tf_op jit(solution)/shard_map/all_to_all | solution.py:157
  22.0 0.0 copy-done
  22.1 1.1 %other_half.1 = bf16[128,16,128]{2,1,0:T(8,128)(2,1)S(1)} custom-call(f32[128,128]{1,0:T(8,128)S(1)} %bitcast.4, bf16[1024,4096]{1,0:T(8,128)(2,1)S(1)} %copy-done), custom_call_target="tpu_custom_call" | custom-call | tf_op jit(solution)/shard_map/other_half/pallas_call | solution.py:163
  23.2 0.0 copy-start.1
  23.2 0.8 %collective-permute-start = (bf16[128,16,128]{2,1,0:T(8,128)(2,1)S(1)}, bf16[128,16,128]{2,1,0:T(8,128)(2,1)S(1)}, u32[]{:S(2)}, u32[]{:S(2)}) collective-permute-start(bf16[128,16,128]{2,1,0:T(8,128)(2,1)S(1)} %other_half.1), channel_id=1, source_target_pairs={{0,16},{16,0},{1,17},{17,1},{2,18},{18,2},{3,19},{19,3},{4,20},{20... | collective-permute-start | bytes 1572872 | tf_op jit(solution)/shard_map/ppermute | solution.py:172
  24.0 1.2 %own_half.1.kept_ref = f32[128,16,128]{2,1,0:T(8,128)S(1)} custom-call(f32[128,128]{1,0:T(8,128)S(1)} %bitcast.5, bf16[1024,4096]{1,0:T(8,128)(2,1)S(1)} %copy-done), custom_call_target="tpu_custom_call" | custom-call | tf_op jit(solution)/shard_map/own_half/pallas_call | solution.py:163
  25.2 0.3 collective-permute-done.got_ref
  25.5 0.1 add.1
  25.6 17.2 %all_to_all.11.got_ref = bf16[128,16,128]{2,1,0:T(8,128)(2,1)S(1)} all-to-all(bf16[128,16,128]{2,1,0:T(8,128)(2,1)S(1)} %add.1), channel_id=1, replica_groups=mesh['y'=4,'core'=2,'z'=4,'x'=4] {'core','x','z','y'}, dimensions={0} | all-to-all | bytes 1048576 | tf_op jit(solution)/shard_map/all_to_all | solution.py:174
  42.8 0.0 copy-done.1
  42.8 0.7 %sum.1 = bf16[1,4096]{1,0:T(2,128)(2,1)} custom-call(bf16[128,16,128]{2,1,0:T(8,128)(2,1)S(1)} %all_to_all.11.got_ref, bf16[1,4096]{1,0:T(2,128)(2,1)S(1)} %copy-done.1), custom_call_target="tpu_custom_call" | custom-call | tf_op jit(solution)/shard_map/sum/pallas_call | solution.py:175
Async XLA Ops:
  0.0 22.1 %copy-start = (bf16[1024,4096]{1,0:T(8,128)(2,1)S(1)}, bf16[1024,4096]{1,0:T(8,128)(2,1)}, u32[]{:S(2)}) copy-start(bf16[1024,4096]{1,0:T(8,128)(2,1)} %refs_1_.5) | copy-start | bytes 25165828
  23.2 19.7 %copy-start.1 = (bf16[1,4096]{1,0:T(2,128)(2,1)S(1)}, bf16[1,4096]{1,0:T(2,128)(2,1)}, u32[]{:S(2)}) copy-start(bf16[1,4096]{1,0:T(2,128)(2,1)} %inputs_ref.1) | copy-start | bytes 24580
  23.2 2.3 %collective-permute-start = (bf16[128,16,128]{2,1,0:T(8,128)(2,1)S(1)}, bf16[128,16,128]{2,1,0:T(8,128)(2,1)S(1)}, u32[]{:S(2)}, u32[]{:S(2)}) collective-permute-start(bf16[128,16,128]{2,1,0:T(8,128)(2,1)S(1)} %other_half.1), channel_id=1, source_target_pairs={{0,16},{16,0},{1,17},{17,1},{2,18},{18,2},{3,19},{19,3},{4,20},{20... | collective-permute-start | bytes 1572872 | tf_op jit(solution)/shard_map/ppermute | solution.py:172

commit v3 on v2

--- a/solution.py
+++ b/solution.py
@@ -79,12 +79,12 @@
 
         rows = [spread(c) + spread(cap + c) for c in range(cap)]
         scales = [spread(2 * cap + c) for c in range(cap)]
-        scales = [
-            sum(jnp.where(rows[c] == rows[d], scales[d], 0.0) for d in range(cap)).astype(
-                jnp.bfloat16
-            )
-            for c in range(cap)
-        ]
+        same = {(c, d): rows[c] == rows[d] for d in range(cap) for c in range(d)}
+        totals = list(scales)
+        for (c, d), match in same.items():
+            totals[c] = totals[c] + jnp.where(match, scales[d], 0.0)
+            totals[d] = totals[d] + jnp.where(match, scales[c], 0.0)
+        scales = [total.astype(jnp.bfloat16) for total in totals]
         rows = [row.astype(jnp.int32).astype(jnp.int16) for row in rows]
         lane = lax.broadcasted_iota(jnp.int32, (group, LANES), 1)
         for k in range(slot_dev // LANES):

time: 43.7 us -> 43.6 us (level)
  no operation moved by 1% of the time
where the time goes in v3:
time: 43.6 us; the launch traced here: 43.5 us
  blocking collectives  38 us (87%)
  Pallas kernels  4.32 us (10%)
  starting transfers between devices  0.81 us (2%)
    all_to_all x1, blocking collectives, body(): lax.all_to_all(packed.reshape(owners, 1, LANES), GROUP, split_axis=0, con...  20.8 us
    all_to_all x1, blocking collectives, body(): lax.all_to_all(partials, GROUP, split_axis=0, concat_axis=0, tiled=True)  17.2 us
    pallas_call x2, Pallas kernels, body(): call(lambda *refs, other=other: half_kernel(cap, chunk, other, *refs), [(...  2.27 us
    pallas_call x1, Pallas kernels, body(): call(lambda *refs: request_kernel(owners, cap, *refs), [((owners, LANES),...  1.27 us
  transfers between devices with their start and end apart: 1, of which 1 were waited for; matrix products, arithmetic and copies ran while one was open for 0% of the time, Pallas kernels for 3%

profile of v3, /device:TPU:1, one launch (start us, length us, event | category | flops | bytes accessed | tf_op | source)
XLA Modules:
  0.0 43.5 jit_solution(6111683099334346189)
XLA Ops:
  0.0 0.0 copy-start
  0.0 1.3 %request.1 = f32[128,128]{1,0:T(8,128)S(1)} custom-call(s32[1,4,32]{2,1,0:T(4,128)} %refs_0_.1, bf16[1,4,32]{2,1,0:T(4,128)(2,1)} %refs_1_.3, bf16[1024,4096]{1,0:T(8,128)(2,1)} %refs_1_.5), custom_call_target="tpu_custom_call" | custom-call | tf_op jit(solution)/shard_map/request/pallas_call | solution.py:146
  1.3 20.8 %all_to_all.10 = f32[128,1,128]{2,1,0:T(1,128)S(1)} all-to-all(f32[128,1,128]{2,1,0:T(1,128)S(1)} %bitcast.6), channel_id=1, replica_groups=mesh['y'=4,'core'=2,'z'=4,'x'=4] {'core','x','z','y'}, dimensions={0} | all-to-all | bytes 131072 | tf_op jit(solution)/shard_map/all_to_all | solution.py:157
  22.0 0.0 copy-done
  22.1 1.1 %other_half.1 = bf16[128,16,128]{2,1,0:T(8,128)(2,1)S(1)} custom-call(f32[128,128]{1,0:T(8,128)S(1)} %bitcast.4, bf16[1024,4096]{1,0:T(8,128)(2,1)S(1)} %copy-done), custom_call_target="tpu_custom_call" | custom-call | tf_op jit(solution)/shard_map/other_half/pallas_call | solution.py:163
  23.1 0.0 copy-start.1
  23.2 0.8 %collective-permute-start = (bf16[128,16,128]{2,1,0:T(8,128)(2,1)S(1)}, bf16[128,16,128]{2,1,0:T(8,128)(2,1)S(1)}, u32[]{:S(2)}, u32[]{:S(2)}) collective-permute-start(bf16[128,16,128]{2,1,0:T(8,128)(2,1)S(1)} %other_half.1), channel_id=1, source_target_pairs={{0,16},{16,0},{1,17},{17,1},{2,18},{18,2},{3,19},{19,3},{4,20},{20... | collective-permute-start | bytes 1572872 | tf_op jit(solution)/shard_map/ppermute | solution.py:172
  24.0 1.2 %own_half.1.kept_ref = f32[128,16,128]{2,1,0:T(8,128)S(1)} custom-call(f32[128,128]{1,0:T(8,128)S(1)} %bitcast.5, bf16[1024,4096]{1,0:T(8,128)(2,1)S(1)} %copy-done), custom_call_target="tpu_custom_call" | custom-call | tf_op jit(solution)/shard_map/own_half/pallas_call | solution.py:163
  25.2 0.3 collective-permute-done.got_ref
  25.5 0.1 add.1
  25.6 17.2 %all_to_all.11.got_ref = bf16[128,16,128]{2,1,0:T(8,128)(2,1)S(1)} all-to-all(bf16[128,16,128]{2,1,0:T(8,128)(2,1)S(1)} %add.1), channel_id=1, replica_groups=mesh['y'=4,'core'=2,'z'=4,'x'=4] {'core','x','z','y'}, dimensions={0} | all-to-all | bytes 1048576 | tf_op jit(solution)/shard_map/all_to_all | solution.py:174
  42.8 0.0 copy-done.1
  42.8 0.7 %sum.1 = bf16[1,4096]{1,0:T(2,128)(2,1)} custom-call(bf16[128,16,128]{2,1,0:T(8,128)(2,1)S(1)} %all_to_all.11.got_ref, bf16[1,4096]{1,0:T(2,128)(2,1)S(1)} %copy-done.1), custom_call_target="tpu_custom_call" | custom-call | tf_op jit(solution)/shard_map/sum/pallas_call | solution.py:175
Async XLA Ops:
  0.0 22.1 %copy-start = (bf16[1024,4096]{1,0:T(8,128)(2,1)S(1)}, bf16[1024,4096]{1,0:T(8,128)(2,1)}, u32[]{:S(2)}) copy-start(bf16[1024,4096]{1,0:T(8,128)(2,1)} %refs_1_.5) | copy-start | bytes 25165828
  23.1 19.7 %copy-start.1 = (bf16[1,4096]{1,0:T(2,128)(2,1)S(1)}, bf16[1,4096]{1,0:T(2,128)(2,1)}, u32[]{:S(2)}) copy-start(bf16[1,4096]{1,0:T(2,128)(2,1)} %inputs_ref.1) | copy-start | bytes 24580
  23.2 2.3 %collective-permute-start = (bf16[128,16,128]{2,1,0:T(8,128)(2,1)S(1)}, bf16[128,16,128]{2,1,0:T(8,128)(2,1)S(1)}, u32[]{:S(2)}, u32[]{:S(2)}) collective-permute-start(bf16[128,16,128]{2,1,0:T(8,128)(2,1)S(1)} %other_half.1), channel_id=1, source_target_pairs={{0,16},{16,0},{1,17},{17,1},{2,18},{18,2},{3,19},{19,3},{4,20},{20... | collective-permute-start | bytes 1572872 | tf_op jit(solution)/shard_map/ppermute | solution.py:172

commit v4 on v2

--- a/solution.py
+++ b/solution.py
@@ -70,15 +70,21 @@
     sources = got_ref.shape[0]
     core = lax.axis_index("core")
     core = 1 - core if other else core
+    field = lax.broadcasted_iota(jnp.int32, (LANES, 2 * cap * LANES), 0)
+    block = lax.broadcasted_iota(jnp.int32, (LANES, 2 * cap * LANES), 1) // LANES
+    wanted = (field == block + cap) | ((field == block) & (block < cap))
+    spread = jnp.dot(
+        got_ref[...].astype(jnp.bfloat16),
+        jnp.where(wanted, 1.0, 0.0).astype(jnp.bfloat16),
+        preferred_element_type=jnp.float32,
+    )
     group = 16
     for n in range(sources // group):
-        got = got_ref[pl.ds(n * group, group)]
-
-        def spread(lane):
-            return jnp.broadcast_to(got[:, lane : lane + 1], (group, LANES))
-
-        rows = [spread(c) + spread(cap + c) for c in range(cap)]
-        scales = [spread(2 * cap + c) for c in range(cap)]
+        blocks = [
+            spread[n * group : (n + 1) * group, c * LANES : (c + 1) * LANES]
+            for c in range(2 * cap)
+        ]
+        rows, scales = blocks[:cap], blocks[cap:]
         scales = [
             sum(jnp.where(rows[c] == rows[d], scales[d], 0.0) for d in range(cap)).astype(
                 jnp.bfloat16

time: 43.7 us -> 43.6 us (level)
  no operation moved by 1% of the time
where the time goes in v4:
time: 43.6 us; the launch traced here: 43.5 us
  blocking collectives  38 us (87%)
  Pallas kernels  4.23 us (10%)
  starting transfers between devices  0.81 us (2%)
    all_to_all x1, blocking collectives, body(): lax.all_to_all(packed.reshape(owners, 1, LANES), GROUP, split_axis=0, con...  20.8 us
    all_to_all x1, blocking collectives, body(): lax.all_to_all(partials, GROUP, split_axis=0, concat_axis=0, tiled=True)  17.2 us
    pallas_call x2, Pallas kernels, body(): call(lambda *refs, other=other: half_kernel(cap, chunk, other, *refs), [(...  2.17 us
    pallas_call x1, Pallas kernels, body(): call(lambda *refs: request_kernel(owners, cap, *refs), [((owners, LANES),...  1.27 us
  transfers between devices with their start and end apart: 1, of which 1 were waited for; matrix products, arithmetic and copies ran while one was open for 0% of the time, Pallas kernels for 3%

profile of v4, /device:TPU:1, one launch (start us, length us, event | category | flops | bytes accessed | tf_op | source)
XLA Modules:
  0.0 43.5 jit_solution(11954379704689951598)
XLA Ops:
  0.0 0.0 copy-start
  0.0 1.3 %request.1 = f32[128,128]{1,0:T(8,128)S(1)} custom-call(s32[1,4,32]{2,1,0:T(4,128)} %refs_0_.1, bf16[1,4,32]{2,1,0:T(4,128)(2,1)} %refs_1_.3, bf16[1024,4096]{1,0:T(8,128)(2,1)} %refs_1_.5), custom_call_target="tpu_custom_call" | custom-call | tf_op jit(solution)/shard_map/request/pallas_call | solution.py:152
  1.3 20.8 %all_to_all.10 = f32[128,1,128]{2,1,0:T(1,128)S(1)} all-to-all(f32[128,1,128]{2,1,0:T(1,128)S(1)} %bitcast.6), channel_id=1, replica_groups=mesh['y'=4,'core'=2,'z'=4,'x'=4] {'core','x','z','y'}, dimensions={0} | all-to-all | bytes 131072 | tf_op jit(solution)/shard_map/all_to_all | solution.py:163
  22.0 0.0 copy-done
  22.1 1.0 %other_half.1 = bf16[128,16,128]{2,1,0:T(8,128)(2,1)S(1)} custom-call(f32[128,128]{1,0:T(8,128)S(1)} %bitcast.4, bf16[1024,4096]{1,0:T(8,128)(2,1)S(1)} %copy-done), custom_call_target="tpu_custom_call" | custom-call | tf_op jit(solution)/shard_map/other_half/pallas_call | solution.py:169
  23.1 0.0 copy-start.1
  23.1 0.8 %collective-permute-start = (bf16[128,16,128]{2,1,0:T(8,128)(2,1)S(1)}, bf16[128,16,128]{2,1,0:T(8,128)(2,1)S(1)}, u32[]{:S(2)}, u32[]{:S(2)}) collective-permute-start(bf16[128,16,128]{2,1,0:T(8,128)(2,1)S(1)} %other_half.1), channel_id=1, source_target_pairs={{0,16},{16,0},{1,17},{17,1},{2,18},{18,2},{3,19},{19,3},{4,20},{20... | collective-permute-start | bytes 1572872 | tf_op jit(solution)/shard_map/ppermute | solution.py:178
  23.9 1.1 %own_half.1.kept_ref = f32[128,16,128]{2,1,0:T(8,128)S(1)} custom-call(f32[128,128]{1,0:T(8,128)S(1)} %bitcast.5, bf16[1024,4096]{1,0:T(8,128)(2,1)S(1)} %copy-done), custom_call_target="tpu_custom_call" | custom-call | tf_op jit(solution)/shard_map/own_half/pallas_call | solution.py:169
  25.1 0.4 collective-permute-done.got_ref
  25.5 0.1 add.1
  25.6 17.2 %all_to_all.11.got_ref = bf16[128,16,128]{2,1,0:T(8,128)(2,1)S(1)} all-to-all(bf16[128,16,128]{2,1,0:T(8,128)(2,1)S(1)} %add.1), channel_id=1, replica_groups=mesh['y'=4,'core'=2,'z'=4,'x'=4] {'core','x','z','y'}, dimensions={0} | all-to-all | bytes 1048576 | tf_op jit(solution)/shard_map/all_to_all | solution.py:180
  42.8 0.0 copy-done.1
  42.8 0.7 %sum.1 = bf16[1,4096]{1,0:T(2,128)(2,1)} custom-call(bf16[128,16,128]{2,1,0:T(8,128)(2,1)S(1)} %all_to_all.11.got_ref, bf16[1,4096]{1,0:T(2,128)(2,1)S(1)} %copy-done.1), custom_call_target="tpu_custom_call" | custom-call | tf_op jit(solution)/shard_map/sum/pallas_call | solution.py:181
Async XLA Ops:
  0.0 22.1 %copy-start = (bf16[1024,4096]{1,0:T(8,128)(2,1)S(1)}, bf16[1024,4096]{1,0:T(8,128)(2,1)}, u32[]{:S(2)}) copy-start(bf16[1024,4096]{1,0:T(8,128)(2,1)} %refs_1_.5) | copy-start | bytes 25165828
  23.1 19.7 %copy-start.1 = (bf16[1,4096]{1,0:T(2,128)(2,1)S(1)}, bf16[1,4096]{1,0:T(2,128)(2,1)}, u32[]{:S(2)}) copy-start(bf16[1,4096]{1,0:T(2,128)(2,1)} %inputs_ref.1) | copy-start | bytes 24580
  23.1 2.3 %collective-permute-start = (bf16[128,16,128]{2,1,0:T(8,128)(2,1)S(1)}, bf16[128,16,128]{2,1,0:T(8,128)(2,1)S(1)}, u32[]{:S(2)}, u32[]{:S(2)}) collective-permute-start(bf16[128,16,128]{2,1,0:T(8,128)(2,1)S(1)} %other_half.1), channel_id=1, source_target_pairs={{0,16},{16,0},{1,17},{17,1},{2,18},{18,2},{3,19},{19,3},{4,20},{20... | collective-permute-start | bytes 1572872 | tf_op jit(solution)/shard_map/ppermute | solution.py:178

commit v5 on v4

--- a/solution.py
+++ b/solution.py
@@ -85,12 +85,12 @@
             for c in range(2 * cap)
         ]
         rows, scales = blocks[:cap], blocks[cap:]
-        scales = [
-            sum(jnp.where(rows[c] == rows[d], scales[d], 0.0) for d in range(cap)).astype(
-                jnp.bfloat16
-            )
-            for c in range(cap)
-        ]
+        same = {(c, d): rows[c] == rows[d] for d in range(cap) for c in range(d)}
+        totals = list(scales)
+        for (c, d), match in same.items():
+            totals[c] = totals[c] + jnp.where(match, scales[d], 0.0)
+            totals[d] = totals[d] + jnp.where(match, scales[c], 0.0)
+        scales = [total.astype(jnp.bfloat16) for total in totals]
         rows = [row.astype(jnp.int32).astype(jnp.int16) for row in rows]
         lane = lax.broadcasted_iota(jnp.int32, (group, LANES), 1)
         for k in range(slot_dev // LANES):

time: 43.6 us -> 43.6 us (level)
  no operation moved by 1% of the time
where the time goes in v5:
time: 43.6 us; the launch traced here: 43.5 us
  blocking collectives  38 us (87%)
  Pallas kernels  4.21 us (10%)
  starting transfers between devices  0.81 us (2%)
    all_to_all x1, blocking collectives, body(): lax.all_to_all(packed.reshape(owners, 1, LANES), GROUP, split_axis=0, con...  20.8 us
    all_to_all x1, blocking collectives, body(): lax.all_to_all(partials, GROUP, split_axis=0, concat_axis=0, tiled=True)  17.2 us
    pallas_call x2, Pallas kernels, body(): call(lambda *refs, other=other: half_kernel(cap, chunk, other, *refs), [(...  2.15 us
    pallas_call x1, Pallas kernels, body(): call(lambda *refs: request_kernel(owners, cap, *refs), [((owners, LANES),...  1.27 us
  transfers between devices with their start and end apart: 1, of which 1 were waited for; matrix products, arithmetic and copies ran while one was open for 0% of the time, Pallas kernels for 3%

profile of v5, /device:TPU:1, one launch (start us, length us, event | category | flops | bytes accessed | tf_op | source)
XLA Modules:
  0.0 43.5 jit_solution(11629543786567258328)
XLA Ops:
  0.0 0.0 copy-start
  0.0 1.3 %request.1 = f32[128,128]{1,0:T(8,128)S(1)} custom-call(s32[1,4,32]{2,1,0:T(4,128)} %refs_0_.1, bf16[1,4,32]{2,1,0:T(4,128)(2,1)} %refs_1_.3, bf16[1024,4096]{1,0:T(8,128)(2,1)} %refs_1_.5), custom_call_target="tpu_custom_call" | custom-call | tf_op jit(solution)/shard_map/request/pallas_call | solution.py:152
  1.3 20.8 %all_to_all.10 = f32[128,1,128]{2,1,0:T(1,128)S(1)} all-to-all(f32[128,1,128]{2,1,0:T(1,128)S(1)} %bitcast.6), channel_id=1, replica_groups=mesh['y'=4,'core'=2,'z'=4,'x'=4] {'core','x','z','y'}, dimensions={0} | all-to-all | bytes 131072 | tf_op jit(solution)/shard_map/all_to_all | solution.py:163
  22.0 0.0 copy-done
  22.1 1.0 %other_half.1 = bf16[128,16,128]{2,1,0:T(8,128)(2,1)S(1)} custom-call(f32[128,128]{1,0:T(8,128)S(1)} %bitcast.4, bf16[1024,4096]{1,0:T(8,128)(2,1)S(1)} %copy-done), custom_call_target="tpu_custom_call" | custom-call | tf_op jit(solution)/shard_map/other_half/pallas_call | solution.py:169
  23.1 0.0 copy-start.1
  23.1 0.8 %collective-permute-start = (bf16[128,16,128]{2,1,0:T(8,128)(2,1)S(1)}, bf16[128,16,128]{2,1,0:T(8,128)(2,1)S(1)}, u32[]{:S(2)}, u32[]{:S(2)}) collective-permute-start(bf16[128,16,128]{2,1,0:T(8,128)(2,1)S(1)} %other_half.1), channel_id=1, source_target_pairs={{0,16},{16,0},{1,17},{17,1},{2,18},{18,2},{3,19},{19,3},{4,20},{20... | collective-permute-start | bytes 1572872 | tf_op jit(solution)/shard_map/ppermute | solution.py:178
  23.9 1.1 %own_half.1.kept_ref = f32[128,16,128]{2,1,0:T(8,128)S(1)} custom-call(f32[128,128]{1,0:T(8,128)S(1)} %bitcast.5, bf16[1024,4096]{1,0:T(8,128)(2,1)S(1)} %copy-done), custom_call_target="tpu_custom_call" | custom-call | tf_op jit(solution)/shard_map/own_half/pallas_call | solution.py:169
  25.0 0.4 collective-permute-done.got_ref
  25.5 0.1 add.1
  25.5 17.2 %all_to_all.11.got_ref = bf16[128,16,128]{2,1,0:T(8,128)(2,1)S(1)} all-to-all(bf16[128,16,128]{2,1,0:T(8,128)(2,1)S(1)} %add.1), channel_id=1, replica_groups=mesh['y'=4,'core'=2,'z'=4,'x'=4] {'core','x','z','y'}, dimensions={0} | all-to-all | bytes 1048576 | tf_op jit(solution)/shard_map/all_to_all | solution.py:180
  42.8 0.0 copy-done.1
  42.8 0.7 %sum.1 = bf16[1,4096]{1,0:T(2,128)(2,1)} custom-call(bf16[128,16,128]{2,1,0:T(8,128)(2,1)S(1)} %all_to_all.11.got_ref, bf16[1,4096]{1,0:T(2,128)(2,1)S(1)} %copy-done.1), custom_call_target="tpu_custom_call" | custom-call | tf_op jit(solution)/shard_map/sum/pallas_call | solution.py:181
Async XLA Ops:
  0.0 22.1 %copy-start = (bf16[1024,4096]{1,0:T(8,128)(2,1)S(1)}, bf16[1024,4096]{1,0:T(8,128)(2,1)}, u32[]{:S(2)}) copy-start(bf16[1024,4096]{1,0:T(8,128)(2,1)} %refs_1_.5) | copy-start | bytes 25165828
  23.1 19.7 %copy-start.1 = (bf16[1,4096]{1,0:T(2,128)(2,1)S(1)}, bf16[1,4096]{1,0:T(2,128)(2,1)}, u32[]{:S(2)}) copy-start(bf16[1,4096]{1,0:T(2,128)(2,1)} %inputs_ref.1) | copy-start | bytes 24580
  23.1 2.3 %collective-permute-start = (bf16[128,16,128]{2,1,0:T(8,128)(2,1)S(1)}, bf16[128,16,128]{2,1,0:T(8,128)(2,1)S(1)}, u32[]{:S(2)}, u32[]{:S(2)}) collective-permute-start(bf16[128,16,128]{2,1,0:T(8,128)(2,1)S(1)} %other_half.1), channel_id=1, source_target_pairs={{0,16},{16,0},{1,17},{17,1},{2,18},{18,2},{3,19},{19,3},{4,20},{20... | collective-permute-start | bytes 1572872 | tf_op jit(solution)/shard_map/ppermute | solution.py:178

commit v6 on v5

--- a/solution.py
+++ b/solution.py
@@ -78,7 +78,9 @@
         jnp.where(wanted, 1.0, 0.0).astype(jnp.bfloat16),
         preferred_element_type=jnp.float32,
     )
-    group = 16
+    group = 32
+    lane = lax.broadcasted_iota(jnp.int32, (group, LANES), 1)
+    places = [(lane + k).astype(jnp.int16) for k in range(0, slot_dev, LANES)]
     for n in range(sources // group):
         blocks = [
             spread[n * group : (n + 1) * group, c * LANES : (c + 1) * LANES]
@@ -92,9 +94,7 @@
             totals[d] = totals[d] + jnp.where(match, scales[c], 0.0)
         scales = [total.astype(jnp.bfloat16) for total in totals]
         rows = [row.astype(jnp.int32).astype(jnp.int16) for row in rows]
-        lane = lax.broadcasted_iota(jnp.int32, (group, LANES), 1)
-        for k in range(slot_dev // LANES):
-            at = (lane + k * LANES).astype(jnp.int16)
+        for k, at in enumerate(places):
             weight = jnp.zeros((group, LANES), jnp.bfloat16)
             for c in range(cap):
                 weight = jnp.where(at == rows[c], scales[c], weight)

time: 43.6 us -> 43.6 us (level)
  no operation moved by 1% of the time
where the time goes in v6:
time: 43.6 us; the launch traced here: 43.5 us
  blocking collectives  38 us (87%)
  Pallas kernels  4.21 us (10%)
  starting transfers between devices  0.81 us (2%)
    all_to_all x1, blocking collectives, body(): lax.all_to_all(packed.reshape(owners, 1, LANES), GROUP, split_axis=0, con...  20.8 us
    all_to_all x1, blocking collectives, body(): lax.all_to_all(partials, GROUP, split_axis=0, concat_axis=0, tiled=True)  17.2 us
    pallas_call x2, Pallas kernels, body(): call(lambda *refs, other=other: half_kernel(cap, chunk, other, *refs), [(...  2.15 us
    pallas_call x1, Pallas kernels, body(): call(lambda *refs: request_kernel(owners, cap, *refs), [((owners, LANES),...  1.27 us
  transfers between devices with their start and end apart: 1, of which 1 were waited for; matrix products, arithmetic and copies ran while one was open for 0% of the time, Pallas kernels for 3%

profile of v6, /device:TPU:1, one launch (start us, length us, event | category | flops | bytes accessed | tf_op | source)
XLA Modules:
  0.0 43.5 jit_solution(11629543786567258328)
XLA Ops:
  0.0 0.0 copy-start
  0.0 1.3 %request.1 = f32[128,128]{1,0:T(8,128)S(1)} custom-call(s32[1,4,32]{2,1,0:T(4,128)} %refs_0_.1, bf16[1,4,32]{2,1,0:T(4,128)(2,1)} %refs_1_.3, bf16[1024,4096]{1,0:T(8,128)(2,1)} %refs_1_.5), custom_call_target="tpu_custom_call" | custom-call | tf_op jit(solution)/shard_map/request/pallas_call | solution.py:152
  1.3 20.8 %all_to_all.10 = f32[128,1,128]{2,1,0:T(1,128)S(1)} all-to-all(f32[128,1,128]{2,1,0:T(1,128)S(1)} %bitcast.6), channel_id=1, replica_groups=mesh['y'=4,'core'=2,'z'=4,'x'=4] {'core','x','z','y'}, dimensions={0} | all-to-all | bytes 131072 | tf_op jit(solution)/shard_map/all_to_all | solution.py:163
  22.0 0.0 copy-done
  22.1 1.0 %other_half.1 = bf16[128,16,128]{2,1,0:T(8,128)(2,1)S(1)} custom-call(f32[128,128]{1,0:T(8,128)S(1)} %bitcast.4, bf16[1024,4096]{1,0:T(8,128)(2,1)S(1)} %copy-done), custom_call_target="tpu_custom_call" | custom-call | tf_op jit(solution)/shard_map/other_half/pallas_call | solution.py:169
  23.1 0.0 copy-start.1
  23.1 0.8 %collective-permute-start = (bf16[128,16,128]{2,1,0:T(8,128)(2,1)S(1)}, bf16[128,16,128]{2,1,0:T(8,128)(2,1)S(1)}, u32[]{:S(2)}, u32[]{:S(2)}) collective-permute-start(bf16[128,16,128]{2,1,0:T(8,128)(2,1)S(1)} %other_half.1), channel_id=1, source_target_pairs={{0,16},{16,0},{1,17},{17,1},{2,18},{18,2},{3,19},{19,3},{4,20},{20... | collective-permute-start | bytes 1572872 | tf_op jit(solution)/shard_map/ppermute | solution.py:178
  23.9 1.1 %own_half.1.kept_ref = f32[128,16,128]{2,1,0:T(8,128)S(1)} custom-call(f32[128,128]{1,0:T(8,128)S(1)} %bitcast.5, bf16[1024,4096]{1,0:T(8,128)(2,1)S(1)} %copy-done), custom_call_target="tpu_custom_call" | custom-call | tf_op jit(solution)/shard_map/own_half/pallas_call | solution.py:169
  25.0 0.4 collective-permute-done.got_ref
  25.5 0.1 add.1
  25.5 17.2 %all_to_all.11.got_ref = bf16[128,16,128]{2,1,0:T(8,128)(2,1)S(1)} all-to-all(bf16[128,16,128]{2,1,0:T(8,128)(2,1)S(1)} %add.1), channel_id=1, replica_groups=mesh['y'=4,'core'=2,'z'=4,'x'=4] {'core','x','z','y'}, dimensions={0} | all-to-all | bytes 1048576 | tf_op jit(solution)/shard_map/all_to_all | solution.py:180
  42.8 0.0 copy-done.1
  42.8 0.7 %sum.1 = bf16[1,4096]{1,0:T(2,128)(2,1)} custom-call(bf16[128,16,128]{2,1,0:T(8,128)(2,1)S(1)} %all_to_all.11.got_ref, bf16[1,4096]{1,0:T(2,128)(2,1)S(1)} %copy-done.1), custom_call_target="tpu_custom_call" | custom-call | tf_op jit(solution)/shard_map/sum/pallas_call | solution.py:181
Async XLA Ops:
  0.0 22.1 %copy-start = (bf16[1024,4096]{1,0:T(8,128)(2,1)S(1)}, bf16[1024,4096]{1,0:T(8,128)(2,1)}, u32[]{:S(2)}) copy-start(bf16[1024,4096]{1,0:T(8,128)(2,1)} %refs_1_.5) | copy-start | bytes 25165828
  23.1 19.7 %copy-start.1 = (bf16[1,4096]{1,0:T(2,128)(2,1)S(1)}, bf16[1,4096]{1,0:T(2,128)(2,1)}, u32[]{:S(2)}) copy-start(bf16[1,4096]{1,0:T(2,128)(2,1)} %inputs_ref.1) | copy-start | bytes 24580
  23.1 2.3 %collective-permute-start = (bf16[128,16,128]{2,1,0:T(8,128)(2,1)S(1)}, bf16[128,16,128]{2,1,0:T(8,128)(2,1)S(1)}, u32[]{:S(2)}, u32[]{:S(2)}) collective-permute-start(bf16[128,16,128]{2,1,0:T(8,128)(2,1)S(1)} %other_half.1), channel_id=1, source_target_pairs={{0,16},{16,0},{1,17},{17,1},{2,18},{18,2},{3,19},{19,3},{4,20},{20... | collective-permute-start | bytes 1572872 | tf_op jit(solution)/shard_map/ppermute | solution.py:178

commit v7 on v5

--- a/solution.py
+++ b/solution.py
@@ -70,11 +70,12 @@
     sources = got_ref.shape[0]
     core = lax.axis_index("core")
     core = 1 - core if other else core
-    field = lax.broadcasted_iota(jnp.int32, (LANES, 2 * cap * LANES), 0)
-    block = lax.broadcasted_iota(jnp.int32, (LANES, 2 * cap * LANES), 1) // LANES
+    fields = 4 * cap
+    field = lax.broadcasted_iota(jnp.int32, (fields, 2 * cap * LANES), 0)
+    block = lax.broadcasted_iota(jnp.int32, (fields, 2 * cap * LANES), 1) // LANES
     wanted = (field == block + cap) | ((field == block) & (block < cap))
     spread = jnp.dot(
-        got_ref[...].astype(jnp.bfloat16),
+        got_ref[:, :fields].astype(jnp.bfloat16),
         jnp.where(wanted, 1.0, 0.0).astype(jnp.bfloat16),
         preferred_element_type=jnp.float32,
     )

time: 43.6 us -> 43.6 us (level)
  no operation moved by 1% of the time
where the time goes in v7:
time: 43.6 us; the launch traced here: 43.5 us
  blocking collectives  38 us (87%)
  Pallas kernels  4.18 us (10%)
  starting transfers between devices  0.81 us (2%)
    all_to_all x1, blocking collectives, body(): lax.all_to_all(packed.reshape(owners, 1, LANES), GROUP, split_axis=0, con...  20.8 us
    all_to_all x1, blocking collectives, body(): lax.all_to_all(partials, GROUP, split_axis=0, concat_axis=0, tiled=True)  17.2 us
    pallas_call x2, Pallas kernels, body(): call(lambda *refs, other=other: half_kernel(cap, chunk, other, *refs), [(...  2.12 us
    pallas_call x1, Pallas kernels, body(): call(lambda *refs: request_kernel(owners, cap, *refs), [((owners, LANES),...  1.27 us
  transfers between devices with their start and end apart: 1, of which 1 were waited for; matrix products, arithmetic and copies ran while one was open for 0% of the time, Pallas kernels for 3%

profile of v7, /device:TPU:1, one launch (start us, length us, event | category | flops | bytes accessed | tf_op | source)
XLA Modules:
  0.0 43.5 jit_solution(14865639974316367482)
XLA Ops:
  0.0 0.0 copy-start
  0.0 1.3 %request.1 = f32[128,128]{1,0:T(8,128)S(1)} custom-call(s32[1,4,32]{2,1,0:T(4,128)} %refs_0_.1, bf16[1,4,32]{2,1,0:T(4,128)(2,1)} %refs_1_.3, bf16[1024,4096]{1,0:T(8,128)(2,1)} %refs_1_.5), custom_call_target="tpu_custom_call" | custom-call | tf_op jit(solution)/shard_map/request/pallas_call | solution.py:153
  1.3 20.8 %all_to_all.10 = f32[128,1,128]{2,1,0:T(1,128)S(1)} all-to-all(f32[128,1,128]{2,1,0:T(1,128)S(1)} %bitcast.6), channel_id=1, replica_groups=mesh['y'=4,'core'=2,'z'=4,'x'=4] {'core','x','z','y'}, dimensions={0} | all-to-all | bytes 131072 | tf_op jit(solution)/shard_map/all_to_all | solution.py:164
  22.0 0.0 copy-done
  22.1 1.0 %other_half.1 = bf16[128,16,128]{2,1,0:T(8,128)(2,1)S(1)} custom-call(f32[128,128]{1,0:T(8,128)S(1)} %bitcast.4, bf16[1024,4096]{1,0:T(8,128)(2,1)S(1)} %copy-done), custom_call_target="tpu_custom_call" | custom-call | tf_op jit(solution)/shard_map/other_half/pallas_call | solution.py:170
  23.1 0.0 copy-start.1
  23.1 0.8 %collective-permute-start = (bf16[128,16,128]{2,1,0:T(8,128)(2,1)S(1)}, bf16[128,16,128]{2,1,0:T(8,128)(2,1)S(1)}, u32[]{:S(2)}, u32[]{:S(2)}) collective-permute-start(bf16[128,16,128]{2,1,0:T(8,128)(2,1)S(1)} %other_half.1), channel_id=1, source_target_pairs={{0,16},{16,0},{1,17},{17,1},{2,18},{18,2},{3,19},{19,3},{4,20},{20... | collective-permute-start | bytes 1572872 | tf_op jit(solution)/shard_map/ppermute | solution.py:179
  23.9 1.1 %own_half.1.kept_ref = f32[128,16,128]{2,1,0:T(8,128)S(1)} custom-call(f32[128,128]{1,0:T(8,128)S(1)} %bitcast.5, bf16[1024,4096]{1,0:T(8,128)(2,1)S(1)} %copy-done), custom_call_target="tpu_custom_call" | custom-call | tf_op jit(solution)/shard_map/own_half/pallas_call | solution.py:170
  25.0 0.4 collective-permute-done.got_ref
  25.4 0.1 add.1
  25.5 17.2 %all_to_all.11.got_ref = bf16[128,16,128]{2,1,0:T(8,128)(2,1)S(1)} all-to-all(bf16[128,16,128]{2,1,0:T(8,128)(2,1)S(1)} %add.1), channel_id=1, replica_groups=mesh['y'=4,'core'=2,'z'=4,'x'=4] {'core','x','z','y'}, dimensions={0} | all-to-all | bytes 1048576 | tf_op jit(solution)/shard_map/all_to_all | solution.py:181
  42.8 0.0 copy-done.1
  42.8 0.7 %sum.1 = bf16[1,4096]{1,0:T(2,128)(2,1)} custom-call(bf16[128,16,128]{2,1,0:T(8,128)(2,1)S(1)} %all_to_all.11.got_ref, bf16[1,4096]{1,0:T(2,128)(2,1)S(1)} %copy-done.1), custom_call_target="tpu_custom_call" | custom-call | tf_op jit(solution)/shard_map/sum/pallas_call | solution.py:182
Async XLA Ops:
  0.0 22.1 %copy-start = (bf16[1024,4096]{1,0:T(8,128)(2,1)S(1)}, bf16[1024,4096]{1,0:T(8,128)(2,1)}, u32[]{:S(2)}) copy-start(bf16[1024,4096]{1,0:T(8,128)(2,1)} %refs_1_.5) | copy-start | bytes 25165828
  23.1 19.7 %copy-start.1 = (bf16[1,4096]{1,0:T(2,128)(2,1)S(1)}, bf16[1,4096]{1,0:T(2,128)(2,1)}, u32[]{:S(2)}) copy-start(bf16[1,4096]{1,0:T(2,128)(2,1)} %inputs_ref.1) | copy-start | bytes 24580
  23.1 2.3 %collective-permute-start = (bf16[128,16,128]{2,1,0:T(8,128)(2,1)S(1)}, bf16[128,16,128]{2,1,0:T(8,128)(2,1)S(1)}, u32[]{:S(2)}, u32[]{:S(2)}) collective-permute-start(bf16[128,16,128]{2,1,0:T(8,128)(2,1)S(1)} %other_half.1), channel_id=1, source_target_pairs={{0,16},{16,0},{1,17},{17,1},{2,18},{18,2},{3,19},{19,3},{4,20},{20... | collective-permute-start | bytes 1572872 | tf_op jit(solution)/shard_map/ppermute | solution.py:179

commit v8 on v7

--- a/solution.py
+++ b/solution.py
@@ -49,7 +49,7 @@
         preferred_element_type=jnp.float32,
     )
     rank = jnp.sum(jnp.where(mine, earlier, 0.0), axis=0, keepdims=True).astype(jnp.int32)
-    lane = lax.broadcasted_iota(jnp.int32, (LANES, picks), 0) - rank
+    lane = lax.broadcasted_iota(jnp.int32, (4 * cap, picks), 0) - rank
     fields = jnp.where(
         lane == 0,
         high.astype(jnp.float32),
@@ -57,12 +57,14 @@
             lane == cap, low.astype(jnp.float32), jnp.where(lane == 2 * cap, weights, 0.0)
         ),
     )
-    out_ref[...] = lax.dot_general(
+    total = lax.dot_general(
         marks,
         fields.astype(jnp.bfloat16),
         (((1,), (1,)), ((), ())),
         preferred_element_type=jnp.float32,
     )
+    rest = jnp.zeros((owners, LANES - 4 * cap), jnp.float32)
+    out_ref[...] = jnp.concatenate([total, rest], axis=1)
 
 
 def half_kernel(cap, chunk, other, got_ref, slab_ref, out_ref, table):

time: 43.6 us -> 43.6 us (level)
  no operation moved by 1% of the time
where the time goes in v8:
time: 43.6 us; the launch traced here: 43.4 us
  blocking collectives  38 us (87%)
  Pallas kernels  4.16 us (10%)
  starting transfers between devices  0.81 us (2%)
    all_to_all x1, blocking collectives, body(): lax.all_to_all(packed.reshape(owners, 1, LANES), GROUP, split_axis=0, con...  20.8 us
    all_to_all x1, blocking collectives, body(): lax.all_to_all(partials, GROUP, split_axis=0, concat_axis=0, tiled=True)  17.2 us
    pallas_call x2, Pallas kernels, body(): call(lambda *refs, other=other: half_kernel(cap, chunk, other, *refs), [(...  2.13 us
    pallas_call x1, Pallas kernels, body(): call(lambda *refs: request_kernel(owners, cap, *refs), [((owners, LANES),...  1.24 us
  transfers between devices with their start and end apart: 1, of which 1 were waited for; matrix products, arithmetic and copies ran while one was open for 0% of the time, Pallas kernels for 3%

profile of v8, /device:TPU:1, one launch (start us, length us, event | category | flops | bytes accessed | tf_op | source)
XLA Modules:
  0.0 43.4 jit_solution(6806026757511025010)
XLA Ops:
  0.0 0.0 copy-start
  0.0 1.2 %request.1 = f32[128,128]{1,0:T(8,128)S(1)} custom-call(s32[1,4,32]{2,1,0:T(4,128)} %refs_0_.1, bf16[1,4,32]{2,1,0:T(4,128)(2,1)} %refs_1_.3, bf16[1024,4096]{1,0:T(8,128)(2,1)} %refs_1_.5), custom_call_target="tpu_custom_call" | custom-call | tf_op jit(solution)/shard_map/request/pallas_call | solution.py:155
  1.2 20.8 %all_to_all.10 = f32[128,1,128]{2,1,0:T(1,128)S(1)} all-to-all(f32[128,1,128]{2,1,0:T(1,128)S(1)} %bitcast.6), channel_id=1, replica_groups=mesh['y'=4,'core'=2,'z'=4,'x'=4] {'core','x','z','y'}, dimensions={0} | all-to-all | bytes 131072 | tf_op jit(solution)/shard_map/all_to_all | solution.py:166
  22.0 0.0 copy-done
  22.0 1.0 %other_half.1 = bf16[128,16,128]{2,1,0:T(8,128)(2,1)S(1)} custom-call(f32[128,128]{1,0:T(8,128)S(1)} %bitcast.4, bf16[1024,4096]{1,0:T(8,128)(2,1)S(1)} %copy-done), custom_call_target="tpu_custom_call" | custom-call | tf_op jit(solution)/shard_map/other_half/pallas_call | solution.py:172
  23.1 0.0 copy-start.1
  23.1 0.8 %collective-permute-start = (bf16[128,16,128]{2,1,0:T(8,128)(2,1)S(1)}, bf16[128,16,128]{2,1,0:T(8,128)(2,1)S(1)}, u32[]{:S(2)}, u32[]{:S(2)}) collective-permute-start(bf16[128,16,128]{2,1,0:T(8,128)(2,1)S(1)} %other_half.1), channel_id=1, source_target_pairs={{0,16},{16,0},{1,17},{17,1},{2,18},{18,2},{3,19},{19,3},{4,20},{20... | collective-permute-start | bytes 1572872 | tf_op jit(solution)/shard_map/ppermute | solution.py:181
  23.9 1.1 %own_half.1.kept_ref = f32[128,16,128]{2,1,0:T(8,128)S(1)} custom-call(f32[128,128]{1,0:T(8,128)S(1)} %bitcast.5, bf16[1024,4096]{1,0:T(8,128)(2,1)S(1)} %copy-done), custom_call_target="tpu_custom_call" | custom-call | tf_op jit(solution)/shard_map/own_half/pallas_call | solution.py:172
  25.0 0.4 collective-permute-done.got_ref
  25.4 0.1 add.1
  25.5 17.2 %all_to_all.11.got_ref = bf16[128,16,128]{2,1,0:T(8,128)(2,1)S(1)} all-to-all(bf16[128,16,128]{2,1,0:T(8,128)(2,1)S(1)} %add.1), channel_id=1, replica_groups=mesh['y'=4,'core'=2,'z'=4,'x'=4] {'core','x','z','y'}, dimensions={0} | all-to-all | bytes 1048576 | tf_op jit(solution)/shard_map/all_to_all | solution.py:183
  42.7 0.0 copy-done.1
  42.7 0.7 %sum.1 = bf16[1,4096]{1,0:T(2,128)(2,1)} custom-call(bf16[128,16,128]{2,1,0:T(8,128)(2,1)S(1)} %all_to_all.11.got_ref, bf16[1,4096]{1,0:T(2,128)(2,1)S(1)} %copy-done.1), custom_call_target="tpu_custom_call" | custom-call | tf_op jit(solution)/shard_map/sum/pallas_call | solution.py:184
Async XLA Ops:
  0.0 22.0 %copy-start = (bf16[1024,4096]{1,0:T(8,128)(2,1)S(1)}, bf16[1024,4096]{1,0:T(8,128)(2,1)}, u32[]{:S(2)}) copy-start(bf16[1024,4096]{1,0:T(8,128)(2,1)} %refs_1_.5) | copy-start | bytes 25165828
  23.1 19.7 %copy-start.1 = (bf16[1,4096]{1,0:T(2,128)(2,1)S(1)}, bf16[1,4096]{1,0:T(2,128)(2,1)}, u32[]{:S(2)}) copy-start(bf16[1,4096]{1,0:T(2,128)(2,1)} %inputs_ref.1) | copy-start | bytes 24580
  23.1 2.3 %collective-permute-start = (bf16[128,16,128]{2,1,0:T(8,128)(2,1)S(1)}, bf16[128,16,128]{2,1,0:T(8,128)(2,1)S(1)}, u32[]{:S(2)}, u32[]{:S(2)}) collective-permute-start(bf16[128,16,128]{2,1,0:T(8,128)(2,1)S(1)} %other_half.1), channel_id=1, source_target_pairs={{0,16},{16,0},{1,17},{17,1},{2,18},{18,2},{3,19},{19,3},{4,20},{20... | collective-permute-start | bytes 1572872 | tf_op jit(solution)/shard_map/ppermute | solution.py:181

commit v9 on v8

--- a/solution.py
+++ b/solution.py
@@ -120,8 +120,8 @@
     memory = jnp.concatenate(
         [
             sum(
-                jnp.sum(got_ref[pl.ds(core * chips + n, 8)].astype(jnp.float32), axis=0)
-                for n in range(0, chips, 8)
+                jnp.sum(got_ref[pl.ds(core * chips + n, 16)].astype(jnp.float32), axis=0)
+                for n in range(0, chips, 16)
             )
             for core in range(2)
         ],

time: 43.6 us -> 43.6 us (level)
  no operation moved by 1% of the time
where the time goes in v9:
time: 43.6 us; the launch traced here: 43.4 us
  blocking collectives  38 us (87%)
  Pallas kernels  4.16 us (10%)
  starting transfers between devices  0.81 us (2%)
    all_to_all x1, blocking collectives, body(): lax.all_to_all(packed.reshape(owners, 1, LANES), GROUP, split_axis=0, con...  20.8 us
    all_to_all x1, blocking collectives, body(): lax.all_to_all(partials, GROUP, split_axis=0, concat_axis=0, tiled=True)  17.2 us
    pallas_call x2, Pallas kernels, body(): call(lambda *refs, other=other: half_kernel(cap, chunk, other, *refs), [(...  2.13 us
    pallas_call x1, Pallas kernels, body(): call(lambda *refs: request_kernel(owners, cap, *refs), [((owners, LANES),...  1.24 us
  transfers between devices with their start and end apart: 1, of which 1 were waited for; matrix products, arithmetic and copies ran while one was open for 0% of the time, Pallas kernels for 3%

profile of v9, /device:TPU:1, one launch (start us, length us, event | category | flops | bytes accessed | tf_op | source)
XLA Modules:
  0.0 43.4 jit_solution(1658818461870497478)
XLA Ops:
  0.0 0.0 copy-start
  0.0 1.2 %request.1 = f32[128,128]{1,0:T(8,128)S(1)} custom-call(s32[1,4,32]{2,1,0:T(4,128)} %refs_0_.1, bf16[1,4,32]{2,1,0:T(4,128)(2,1)} %refs_1_.3, bf16[1024,4096]{1,0:T(8,128)(2,1)} %refs_1_.5), custom_call_target="tpu_custom_call" | custom-call | tf_op jit(solution)/shard_map/request/pallas_call | solution.py:155
  1.2 20.8 %all_to_all.10 = f32[128,1,128]{2,1,0:T(1,128)S(1)} all-to-all(f32[128,1,128]{2,1,0:T(1,128)S(1)} %bitcast.6), channel_id=1, replica_groups=mesh['y'=4,'core'=2,'z'=4,'x'=4] {'core','x','z','y'}, dimensions={0} | all-to-all | bytes 131072 | tf_op jit(solution)/shard_map/all_to_all | solution.py:166
  22.0 0.0 copy-done
  22.0 1.0 %other_half.1 = bf16[128,16,128]{2,1,0:T(8,128)(2,1)S(1)} custom-call(f32[128,128]{1,0:T(8,128)S(1)} %bitcast.4, bf16[1024,4096]{1,0:T(8,128)(2,1)S(1)} %copy-done), custom_call_target="tpu_custom_call" | custom-call | tf_op jit(solution)/shard_map/other_half/pallas_call | solution.py:172
  23.1 0.0 copy-start.1
  23.1 0.8 %collective-permute-start = (bf16[128,16,128]{2,1,0:T(8,128)(2,1)S(1)}, bf16[128,16,128]{2,1,0:T(8,128)(2,1)S(1)}, u32[]{:S(2)}, u32[]{:S(2)}) collective-permute-start(bf16[128,16,128]{2,1,0:T(8,128)(2,1)S(1)} %other_half.1), channel_id=1, source_target_pairs={{0,16},{16,0},{1,17},{17,1},{2,18},{18,2},{3,19},{19,3},{4,20},{20... | collective-permute-start | bytes 1572872 | tf_op jit(solution)/shard_map/ppermute | solution.py:181
  23.9 1.1 %own_half.1.kept_ref = f32[128,16,128]{2,1,0:T(8,128)S(1)} custom-call(f32[128,128]{1,0:T(8,128)S(1)} %bitcast.5, bf16[1024,4096]{1,0:T(8,128)(2,1)S(1)} %copy-done), custom_call_target="tpu_custom_call" | custom-call | tf_op jit(solution)/shard_map/own_half/pallas_call | solution.py:172
  25.0 0.4 collective-permute-done.got_ref
  25.4 0.1 add.1
  25.5 17.2 %all_to_all.11.got_ref = bf16[128,16,128]{2,1,0:T(8,128)(2,1)S(1)} all-to-all(bf16[128,16,128]{2,1,0:T(8,128)(2,1)S(1)} %add.1), channel_id=1, replica_groups=mesh['y'=4,'core'=2,'z'=4,'x'=4] {'core','x','z','y'}, dimensions={0} | all-to-all | bytes 1048576 | tf_op jit(solution)/shard_map/all_to_all | solution.py:183
  42.7 0.0 copy-done.1
  42.7 0.7 %sum.1 = bf16[1,4096]{1,0:T(2,128)(2,1)} custom-call(bf16[128,16,128]{2,1,0:T(8,128)(2,1)S(1)} %all_to_all.11.got_ref, bf16[1,4096]{1,0:T(2,128)(2,1)S(1)} %copy-done.1), custom_call_target="tpu_custom_call" | custom-call | tf_op jit(solution)/shard_map/sum/pallas_call | solution.py:184
Async XLA Ops:
  0.0 22.0 %copy-start = (bf16[1024,4096]{1,0:T(8,128)(2,1)S(1)}, bf16[1024,4096]{1,0:T(8,128)(2,1)}, u32[]{:S(2)}) copy-start(bf16[1024,4096]{1,0:T(8,128)(2,1)} %refs_1_.5) | copy-start | bytes 25165828
  23.1 19.7 %copy-start.1 = (bf16[1,4096]{1,0:T(2,128)(2,1)S(1)}, bf16[1,4096]{1,0:T(2,128)(2,1)}, u32[]{:S(2)}) copy-start(bf16[1,4096]{1,0:T(2,128)(2,1)} %inputs_ref.1) | copy-start | bytes 24580
  23.1 2.3 %collective-permute-start = (bf16[128,16,128]{2,1,0:T(8,128)(2,1)S(1)}, bf16[128,16,128]{2,1,0:T(8,128)(2,1)S(1)}, u32[]{:S(2)}, u32[]{:S(2)}) collective-permute-start(bf16[128,16,128]{2,1,0:T(8,128)(2,1)S(1)} %other_half.1), channel_id=1, source_target_pairs={{0,16},{16,0},{1,17},{17,1},{2,18},{18,2},{3,19},{19,3},{4,20},{20... | collective-permute-start | bytes 1572872 | tf_op jit(solution)/shard_map/ppermute | solution.py:181
